TPU v7x, 256 devices: a whole 4x4x8 slice. The times are simulated.
256 devices in a mesh: grp: 16 (over y_hi, z), uly: 4 (over x), blk: 4 (over y_lo, core).
Axes of the slice: x: 4, y: 4 (y_hi: 2, y_lo: 2; y = y_hi * 2 + y_lo), z: 8, core: 2. Of those that a mesh axis runs over, the one named last changes fastest.
Arguments:
- q_in: bfloat16 [16, 3072, 2560], P(None, ('grp', 'uly', 'blk')), may hold values from -80 to 80
- k_in: bfloat16 [16, 3072, 2560], P(None, ('grp', 'uly', 'blk')), may hold values from -80 to 80
- v_in: bfloat16 [16, 3072, 2560], P(None, ('grp', 'uly', 'blk')), may hold values from -6 to 6
- q_gain: float32 [2560], replicated, may hold values from 1 to 3
- k_gain: float32 [2560], replicated, may hold values from 1 to 3
- lengths: int32 [16], replicated, may hold values from 1 to 3072, 30720 in all
Outputs:
- attended: bfloat16 [16, 3072, 2560], P(None, ('grp', 'uly', 'blk'))
All inputs are finite; a program needn't handle non-finite values.
Results may differ from a plain program's by a relative error of at most 0.012.
The roundings to bfloat16 on the way count: a program that leaves them out, or rounds other values in their place, can miss the bound.
Values may be sent and summed in bfloat16 or wider, within the bound.
A program may use at most 128 MiB of HBM per device.

v0:
```python
import jax
import jax.numpy as jnp
from jax import lax
from jax.sharding import PartitionSpec as P

HD = 128


def rms_scale(values, gain):
    wide = values.astype(jnp.float32)
    power = jnp.mean(wide * wide, axis=-1, keepdims=True)
    return (wide * lax.rsqrt(power + 1e-06) * gain).astype(jnp.bfloat16)


def per_device(q_in, k_in, v_in, q_gain, k_gain, lengths):
    stacked = jnp.stack([rms_scale(q_in, q_gain), rms_scale(k_in, k_gain), v_in])
    moved = lax.all_to_all(
        lax.all_to_all(stacked, "grp", split_axis=1, concat_axis=2, tiled=True),
        "uly",
        split_axis=3,
        concat_axis=2,
        tiled=True,
    )
    span = moved.shape[2]
    width = moved.shape[3]
    heads_here = width // HD
    count = lengths[lax.axis_index("grp")]
    offsets = jnp.arange(span, dtype=jnp.int32)
    query_pos = lax.axis_index("blk") * span + offsets
    queries = moved[0, 0].reshape(span, heads_here, HD)
    scale = HD ** (-0.5)
    floor_value = jnp.float32(-1e30)

    def update(carry, key_block, value_block, first):
        rows = key_block.shape[0]
        index = first + jnp.arange(rows, dtype=jnp.int32)
        key_pos = index // span * span + index % span
        key_live = key_pos < count
        top, total, accum = carry
        keys3 = key_block.reshape(rows, heads_here, HD)
        values3 = value_block.reshape(rows, heads_here, HD)
        scores = (
            jnp.einsum("qhd,khd->hqk", queries, keys3, preferred_element_type=jnp.float32) * scale
        )
        scores = jnp.where(key_live[None, None, :], scores, floor_value)
        new_top = jnp.maximum(top, jnp.max(scores, axis=-1))
        shrink = jnp.exp(top - new_top)
        weights = jnp.where(
            key_live[None, None, :], jnp.exp(scores - new_top[..., None]), jnp.float32(0.0)
        )
        new_total = total * shrink + jnp.sum(weights, axis=-1)
        added = jnp.einsum(
            "hqk,khd->hqd",
            weights.astype(jnp.bfloat16),
            values3,
            preferred_element_type=jnp.float32,
        )
        return (new_top, new_total, accum * shrink[..., None] + added)

    initial = (
        jnp.full((heads_here, span), floor_value, jnp.float32),
        jnp.zeros((heads_here, span), jnp.float32),
        jnp.zeros((heads_here, span, HD), jnp.float32),
    )
    key_piece = lax.all_gather(moved[1, 0], "blk", axis=0, tiled=True)
    value_piece = lax.all_gather(moved[2, 0], "blk", axis=0, tiled=True)
    rows = key_piece.shape[0]
    steps = rows // span
    key_stack = key_piece.reshape(steps, span, width)
    value_stack = value_piece.reshape(steps, span, width)
    starts = span * jnp.arange(steps, dtype=jnp.int32)

    def one_step(state, items):
        return (update(state, items[0], items[1], items[2]), None)

    result, unused = lax.scan(one_step, initial, (key_stack, value_stack, starts))
    top, total, accum = result
    mixed = accum / total[..., None]
    joined = jnp.transpose(mixed, (1, 0, 2)).reshape(span, width)
    joined = jnp.where((query_pos < count)[:, None], joined, jnp.float32(0.0)).astype(jnp.bfloat16)
    outgoing = joined[None]
    return lax.all_to_all(
        lax.all_to_all(outgoing, "uly", split_axis=1, concat_axis=2, tiled=True),
        "grp",
        split_axis=1,
        concat_axis=0,
        tiled=True,
    )


def solution(mesh):
    placed = (
        P(None, ("grp", "uly", "blk"), None),
        P(None, ("grp", "uly", "blk"), None),
        P(None, ("grp", "uly", "blk"), None),
        P(),
        P(),
        P(),
    )
    return jax.shard_map(
        per_device,
        mesh=mesh,
        in_specs=placed,
        out_specs=P(None, ("grp", "uly", "blk"), None),
        check_vma=False,
    )
```

profile of v0, /device:TPU:32, one launch (start us, length us, event | category | flops | bytes accessed | tf_op | source)
XLA Modules:
  0.0 496.7 jit_solution(11073818824505770149)
XLA Ops:
  6.6 2.5 fusion.26
  9.1 2.4 fusion.23
  11.4 1.8 copy.68
  13.3 1.4 fusion.30
  15.3 101.5 %all_to_all.58 = bf16[3,16,12,2560]{3,2,0,1:T(8,128)(2,1)S(1)} all-to-all(bf16[3,16,12,2560]{3,2,0,1:T(8,128)(2,1)S(1)} %pad_maximum_fusion), channel_id=1, replica_groups=mesh['grp'=16,'uly'=4,'blk'=4] {'grp'}, dimensions={1} | all-to-all | bytes 5898240 | tf_op jit(solution)/shard_map/all_to_all | solution.py:18
  116.8 2.2 copy.37
  119.0 3.9 all_to_all.43
  122.9 5.8 %copy.38 = bf16[3,1,192,2560]{2,0,1,3:T(4,128)(2,1)} copy(bf16[3,1,192,2560]{3,2,0,1:T(8,128)(2,1)S(1)} %all_to_all.43) | data formatting | bytes 5898240 | tf_op jit(solution)/shard_map/all_to_all | solution.py:18
  128.7 63.5 %all_to_all.59 = bf16[3,1,192,2560]{2,0,1,3:T(4,128)(2,1)} all-to-all(bf16[3,1,192,2560]{2,0,1,3:T(4,128)(2,1)} %copy.38), channel_id=1, replica_groups=mesh['grp'=16,'uly'=4,'blk'=4] {'uly'}, dimensions={3} | all-to-all | bytes 5898240 | tf_op jit(solution)/shard_map/all_to_all | solution.py:17
  192.2 8.8 %copy.54 = bf16[3,1,192,4,640]{4,3,2,0,1:T(4,128)(2,1)S(1)} copy(bf16[3,1,192,4,640]{2,0,4,3,1:T(4,128)(2,1)} %bitcast.71) | data formatting | bytes 5898240 | tf_op jit(solution)/shard_map/all_to_all | solution.py:17
  201.0 2.3 fusion.32
  203.3 1.1 copy.40
  205.0 1.1 copy.42
  206.2 0.7 dynamic_slice.23
  206.8 0.7 add_compare_fusion
  207.5 1.9 copy.41
  209.5 1.2 reshape_squeeze.3
  210.7 1.3 copy.44
  212.0 35.4 %all-gather.3.cloned.1.call-done = bf16[3072,640]{1,0:T(8,128)(2,1)} async-done(((bf16[768,640]{1,0:T(8,128)(2,1)}), bf16[3072,640]{1,0:T(8,128)(2,1)}) %all-gather.3.cloned.1.call-update) | async-done | bytes 3932176 | tf_op jit(solution)/shard_map/all_gather | solution.py:65
  247.4 49.7 %all-gather.5.cloned.1.call-done = bf16[3072,640]{1,0:T(8,128)(2,1)} async-done(((bf16[768,640]{1,0:T(8,128)(2,1)}), bf16[3072,640]{1,0:T(8,128)(2,1)}) %all-gather.5.cloned.1.call-update) | async-done | bytes 3932176 | tf_op jit(solution)/shard_map/all_gather | solution.py:66
  297.1 107.6 %while.17 = (s32[]{:T(128)}, f32[5,768]{1,0:T(8,128)S(1)}, f32[5,768]{1,0:T(8,128)S(1)}, f32[5,768,128]{2,1,0:T(8,128)}, s32[4]{0:T(128)S(1)}, /*index=5*/s32[]{...) while((s32[]{:T(128)}, f32[5,768]{1,0:T(8,128)S(1)}, ...), condition=%wide.region_5.6_spmd.clone, body=%wide.region_2.5_spmd.clone.sunk | while | flops 1549794048 | bytes 50384012 | solution.py:76
  297.1 0.7 dynamic_slice.32
  297.8 1.4 fusion.48
  299.2 1.7 constant_dynamic-slice_fusion.3
  300.8 0.6 copy.71
  301.5 7.0 %bitcast_reduce_fusion.3 = (f32[5,768]{1,0:T(8,128)S(1)}, f32[5,768,768]{2,1,0:T(8,128)}) fusion(pred[768]{0:T(1024)(128)(4,1)S(1)} %fusion.48, bf16[768,5,128]{0,2,1:T(8,128)(2,1)S(1)} %bitcast.69, bf16[768,5,128]{2,0,1:T(8,128)(2,1)} %get-tuple-element.306), kind=kOutput, calls=%fused_computation.1.clone.1 | convolution fusion | flops 763818240 | bytes 13778688 | tf_op jit(solution)/shard_map/while/body/eval_jaxpr/qhd,khd->hqk/dot_general | solution.py:43
  308.5 6.5 %fusion.49 = f32[5,768]{1,0:T(8,128)S(1)} fusion(f32[5,768,768]{2,1,0:T(8,128)} %get-tuple-element.273, f32[5,768]{1,0:T(8,128)S(1)} %select_maximum_fusion.2, pred[768]{0:T(1024)(128)(4,1)S(1)} %fusion.48), kind=kLoop, calls=%fused_computation.6.clone.1 | loop fusion | flops 14741760 | bytes 11827968 | tf_op jit(solution)/shard_map/while/body/eval_jaxpr/reduce_sum | solution.py:51
  315.0 0.6 copy.72
  315.7 8.1 %fusion.51 = f32[5,768,128]{2,1,0:T(8,128)} fusion(f32[5,768,128]{2,1,0:T(8,128)} %get-tuple-element.291, bf16[768,5,128]{0,2,1:T(8,128)(2,1)S(1)} %bitcast.70, f32[5,768,768]{2,1,0:T(8,128)} %get-tuple-element.273, f32[5,768]{1,0:T(8,128)S(1)} %select_maximum_fusion.2, pred[768]{0:T(1024)(128)(4,1)S(1)} %fusion.48, ...), kind=kOutput, calls=%fused_computation.11.clone.1 | convolution fusion | flops 771194880 | bytes 16743169 | tf_op jit(solution)/shard_map/while/body/eval_jaxpr/hqk,khd->hqd/dot_general | solution.py:52
  323.8 0.7 dynamic_slice.32
  324.4 1.4 fusion.48
  325.8 1.7 constant_dynamic-slice_fusion.3
  327.5 0.6 copy.71
  328.2 7.0 %bitcast_reduce_fusion.3 = (f32[5,768]{1,0:T(8,128)S(1)}, f32[5,768,768]{2,1,0:T(8,128)}) fusion(pred[768]{0:T(1024)(128)(4,1)S(1)} %fusion.48, bf16[768,5,128]{0,2,1:T(8,128)(2,1)S(1)} %bitcast.69, bf16[768,5,128]{2,0,1:T(8,128)(2,1)} %get-tuple-element.306), kind=kOutput, calls=%fused_computation.1.clone.1 | convolution fusion | flops 763818240 | bytes 13778688 | tf_op jit(solution)/shard_map/while/body/eval_jaxpr/qhd,khd->hqk/dot_general | solution.py:43
  335.2 6.5 %fusion.49 = f32[5,768]{1,0:T(8,128)S(1)} fusion(f32[5,768,768]{2,1,0:T(8,128)} %get-tuple-element.273, f32[5,768]{1,0:T(8,128)S(1)} %select_maximum_fusion.2, pred[768]{0:T(1024)(128)(4,1)S(1)} %fusion.48), kind=kLoop, calls=%fused_computation.6.clone.1 | loop fusion | flops 14741760 | bytes 11827968 | tf_op jit(solution)/shard_map/while/body/eval_jaxpr/reduce_sum | solution.py:51
  341.7 0.6 copy.72
  342.3 8.4 %fusion.51 = f32[5,768,128]{2,1,0:T(8,128)} fusion(f32[5,768,128]{2,1,0:T(8,128)} %get-tuple-element.291, bf16[768,5,128]{0,2,1:T(8,128)(2,1)S(1)} %bitcast.70, f32[5,768,768]{2,1,0:T(8,128)} %get-tuple-element.273, f32[5,768]{1,0:T(8,128)S(1)} %select_maximum_fusion.2, pred[768]{0:T(1024)(128)(4,1)S(1)} %fusion.48, ...), kind=kOutput, calls=%fused_computation.11.clone.1 | convolution fusion | flops 771194880 | bytes 16743169 | tf_op jit(solution)/shard_map/while/body/eval_jaxpr/hqk,khd->hqd/dot_general | solution.py:52
  350.7 0.7 dynamic_slice.32
  351.4 1.4 fusion.48
  352.8 1.7 constant_dynamic-slice_fusion.3
  354.5 0.6 copy.71
  355.1 7.0 %bitcast_reduce_fusion.3 = (f32[5,768]{1,0:T(8,128)S(1)}, f32[5,768,768]{2,1,0:T(8,128)}) fusion(pred[768]{0:T(1024)(128)(4,1)S(1)} %fusion.48, bf16[768,5,128]{0,2,1:T(8,128)(2,1)S(1)} %bitcast.69, bf16[768,5,128]{2,0,1:T(8,128)(2,1)} %get-tuple-element.306), kind=kOutput, calls=%fused_computation.1.clone.1 | convolution fusion | flops 763818240 | bytes 13778688 | tf_op jit(solution)/shard_map/while/body/eval_jaxpr/qhd,khd->hqk/dot_general | solution.py:43
  362.2 6.5 %fusion.49 = f32[5,768]{1,0:T(8,128)S(1)} fusion(f32[5,768,768]{2,1,0:T(8,128)} %get-tuple-element.273, f32[5,768]{1,0:T(8,128)S(1)} %select_maximum_fusion.2, pred[768]{0:T(1024)(128)(4,1)S(1)} %fusion.48), kind=kLoop, calls=%fused_computation.6.clone.1 | loop fusion | flops 14741760 | bytes 11827968 | tf_op jit(solution)/shard_map/while/body/eval_jaxpr/reduce_sum | solution.py:51
  368.7 0.6 copy.72
  369.3 8.4 %fusion.51 = f32[5,768,128]{2,1,0:T(8,128)} fusion(f32[5,768,128]{2,1,0:T(8,128)} %get-tuple-element.291, bf16[768,5,128]{0,2,1:T(8,128)(2,1)S(1)} %bitcast.70, f32[5,768,768]{2,1,0:T(8,128)} %get-tuple-element.273, f32[5,768]{1,0:T(8,128)S(1)} %select_maximum_fusion.2, pred[768]{0:T(1024)(128)(4,1)S(1)} %fusion.48, ...), kind=kOutput, calls=%fused_computation.11.clone.1 | convolution fusion | flops 771194880 | bytes 16743169 | tf_op jit(solution)/shard_map/while/body/eval_jaxpr/hqk,khd->hqd/dot_general | solution.py:52
  377.7 0.7 dynamic_slice.32
  378.4 1.4 fusion.48
  379.8 1.7 constant_dynamic-slice_fusion.3
  381.5 0.6 copy.71
  382.1 7.0 %bitcast_reduce_fusion.3 = (f32[5,768]{1,0:T(8,128)S(1)}, f32[5,768,768]{2,1,0:T(8,128)}) fusion(pred[768]{0:T(1024)(128)(4,1)S(1)} %fusion.48, bf16[768,5,128]{0,2,1:T(8,128)(2,1)S(1)} %bitcast.69, bf16[768,5,128]{2,0,1:T(8,128)(2,1)} %get-tuple-element.306), kind=kOutput, calls=%fused_computation.1.clone.1 | convolution fusion | flops 763818240 | bytes 13778688 | tf_op jit(solution)/shard_map/while/body/eval_jaxpr/qhd,khd->hqk/dot_general | solution.py:43
  389.2 6.5 %fusion.49 = f32[5,768]{1,0:T(8,128)S(1)} fusion(f32[5,768,768]{2,1,0:T(8,128)} %get-tuple-element.273, f32[5,768]{1,0:T(8,128)S(1)} %select_maximum_fusion.2, pred[768]{0:T(1024)(128)(4,1)S(1)} %fusion.48), kind=kLoop, calls=%fused_computation.6.clone.1 | loop fusion | flops 14741760 | bytes 11827968 | tf_op jit(solution)/shard_map/while/body/eval_jaxpr/reduce_sum | solution.py:51
  395.7 0.6 copy.72
  396.3 8.4 %fusion.51 = f32[5,768,128]{2,1,0:T(8,128)} fusion(f32[5,768,128]{2,1,0:T(8,128)} %get-tuple-element.291, bf16[768,5,128]{0,2,1:T(8,128)(2,1)S(1)} %bitcast.70, f32[5,768,768]{2,1,0:T(8,128)} %get-tuple-element.273, f32[5,768]{1,0:T(8,128)S(1)} %select_maximum_fusion.2, pred[768]{0:T(1024)(128)(4,1)S(1)} %fusion.48, ...), kind=kOutput, calls=%fused_computation.11.clone.1 | convolution fusion | flops 771194880 | bytes 16743169 | tf_op jit(solution)/shard_map/while/body/eval_jaxpr/hqk,khd->hqd/dot_general | solution.py:52
  404.7 1.9 copy.46
  407.0 1.9 copy.47
  409.4 6.6 %reduce.2 = bf16[768,640]{1,0:T(8,128)(2,1)S(1)} reduce(bf16[768,1,640]{2,1,0:T(2,128)(2,1)S(1)} %bitcast.73, bf16[]{:T(256)} %broadcast.207), dimensions={1}, to_apply=%bitcast.41.reduce_sub_computation | reduce | bytes 1966082
  416.3 19.6 %all_to_all.60 = bf16[4,2,61440]{2,1,0:T(2,128)(2,1)S(1)} all-to-all(bf16[4,2,61440]{2,1,0:T(2,128)(2,1)S(1)} %reshape.120), channel_id=1, replica_groups=mesh['grp'=16,'uly'=4,'blk'=4] {'uly'}, dimensions={0} | all-to-all | bytes 1966080 | tf_op jit(solution)/shard_map/all_to_all | solution.py:83
  435.9 0.9 reshape.121
  437.0 0.8 copy.48
  438.3 6.6 %reduce.3 = bf16[192,2560]{1,0:T(8,128)(2,1)S(1)} reduce(bf16[192,1,2560]{2,1,0:T(2,128)(2,1)S(1)} %bitcast.74, bf16[]{:T(256)} %broadcast.207), dimensions={1}, to_apply=%bitcast.43.reduce_sub_computation | reduce | bytes 1966082
  445.4 36.0 %all_to_all.61 = bf16[16,2,15360]{2,1,0:T(2,128)(2,1)S(1)} all-to-all(bf16[16,2,15360]{2,1,0:T(2,128)(2,1)S(1)} %reshape.122), channel_id=1, replica_groups=mesh['grp'=16,'uly'=4,'blk'=4] {'grp'}, dimensions={0} | all-to-all | bytes 1966080 | tf_op jit(solution)/shard_map/all_to_all | solution.py:82
  481.4 0.8 reshape.123
  482.2 5.6 %bitcast_reduce_fusion.1 = bf16[192,2560]{1,0:T(8,128)(2,1)S(1)} fusion(bf16[192,1,2560]{2,1,0:T(2,128)(2,1)S(1)} %reshape.123), kind=kLoop, calls=%fused_computation.55 | loop fusion | bytes 1966080 | tf_op jit(solution)/shard_map/all_to_all | solution.py:82
  488.1 1.5 copy.50
  (45 shorter events, 4.0 us)
Async XLA Ops:
  6.5 6.7 %copy-start = (bf16[16,12,2560]{2,0,1:T(8,128)(2,1)S(1)}, bf16[16,12,2560]{2,0,1:T(8,128)(2,1)}, u32[]{:S(2)}) copy-start(bf16[16,12,2560]{2,0,1:T(8,128)(2,1)} %param.9) | copy-start | bytes 2949124
  6.5 6.7 %copy-start.1 = (bf16[16,12,2560]{2,0,1:T(8,128)(2,1)S(1)}, bf16[16,12,2560]{2,0,1:T(8,128)(2,1)}, u32[]{:S(2)}) copy-start(bf16[16,12,2560]{2,0,1:T(8,128)(2,1)} %param.8) | copy-start | bytes 2949124
  6.5 6.7 %copy-start.5 = (f32[2560]{0:T(1024)S(1)}, f32[2560]{0:T(1024)}, u32[]{:S(2)}) copy-start(f32[2560]{0:T(1024)} %param.11) | copy-start | bytes 30724
  6.5 6.7 %copy-start.4 = (f32[2560]{0:T(1024)S(1)}, f32[2560]{0:T(1024)}, u32[]{:S(2)}) copy-start(f32[2560]{0:T(1024)} %param.12) | copy-start | bytes 30724
  6.5 240.9 %all-gather.3.cloned.1.call-start = ((), (), s32[]{:S(2)}) async-start(), calls=%async_computation.4 | async-start | bytes 4915200 | tf_op jit(solution)/shard_map/all_gather | solution.py:65
  203.3 1.7 copy-start.3
  203.3 2.9 copy-start.6
  203.3 4.2 copy-start.2
  204.4 92.7 %all-gather.5.cloned.1.call-start = ((), (), s32[]{:S(2)}) async-start(), calls=%async_computation.5 | async-start | bytes 4915200 | tf_op jit(solution)/shard_map/all_gather | solution.py:66
Sparse Core Ops, SparseCore 0:
  204.5 42.8 all-gather.2
  249.2 47.8 all-gather.4
where the time goes:
time: 504 us; the launch traced here: 497 us
  blocking collectives  221 us (44%)
  waiting for transfers between devices  85.1 us (17%)
  local copies, waits for them, and re-layouts  62.2 us (12%)
  matrix products  61.3 us (12%)
  other arithmetic  52.8 us (10%)
  between operations  13.9 us (3%)
    all_to_all x1, blocking collectives, per_device(): lax.all_to_all(stacked, 'grp', split_axis=1, concat_axis=2, tiled=True)  101 us
    all_to_all x1, blocking collectives, per_device(): lax.all_to_all(lax.all_to_all(stacked, 'grp', split_axis=1, concat_axis=2...  63.5 us
    all_gather x1, waiting for transfers between devices, per_device(): value_piece = lax.all_gather(moved[2, 0], 'blk', axis=0, tiled=True)  49.7 us
    all_to_all x1, blocking collectives, per_device(): lax.all_to_all(lax.all_to_all(outgoing, 'uly', split_axis=1, concat_axis=...  36 us
    all_gather x1, waiting for transfers between devices, per_device(): key_piece = lax.all_gather(moved[1, 0], 'blk', axis=0, tiled=True)  35.4 us
    dot_general x4, matrix products, update(): jnp.einsum('hqk,khd->hqd', weights.astype(jnp.bfloat16), values3, preferr...  33.3 us
    dot_general x4, matrix products, update(): jnp.einsum('qhd,khd->hqk', queries, keys3, preferred_element_type=jnp.flo...  28.1 us
    reduce_sum x4, other arithmetic, update(): new_total = total * shrink + jnp.sum(weights, axis=-1)  25.9 us
  transfers between devices with their start and end apart: 2, of which 2 were waited for; matrix products, arithmetic and copies ran while one was open for 1% of the time, Pallas kernels for 0%

commit v1 on v0

v1 whole, which is shorter than its diff:
```python
import functools
import math

import jax
import jax.numpy as jnp
from jax import lax
from jax.experimental import pallas as pl
from jax.experimental.pallas import tpu as pltpu
from jax.sharding import PartitionSpec as P

HD = 128
T = 12
R = 16
HALF = 1280
SLOTS = 64
KEYS = 3072
TILE = 384
LOG2E = math.log2(math.e)
MESH = pl.DeviceIdType.MESH
BF = jnp.bfloat16
F32 = jnp.float32


def slot_pos(shape, slot, zpar):
    w = lax.broadcasted_iota(jnp.int32, shape, 1)
    cc = (w >= T).astype(jnp.int32)
    t = w - T * cc
    yl = slot & 1
    x = (slot >> 1) & 3
    zh = (slot >> 3) & 3
    yh = slot >> 5
    z = zh * 2 + zpar
    return ((((yl * 2 + cc) * 4 + x) * 2 + yh) * 8 + z) * T + t


def kernel(
    len_ref, q_ref, k_ref, v_ref, qg_ref, kg_ref, out_ref,
    halves, mates, perm, sb, ss, rb, rsh, rm, rmsh, ka, va, scr, prb, of,
    obs, oshs, ob, osh, fin,
    ex_s, ex_r, main_s, main_r, fwd_s, fwd_r, sh_s, sh_same, sh_other, fsh_s, fsh_r,
    o_s, o_r, osh_s, osh_r, fin_s, fin_r, fin_l,
):
    g = lax.axis_index("grp")
    x = lax.axis_index("uly")
    blk = lax.axis_index("blk")
    c = blk % 2
    yl = blk // 2
    z = g % 8
    yh = g // 8
    zp = z % 2
    zh = z // 2
    slot = ((yh * 4 + zh) * 4 + x) * 2 + yl
    sgrp = slot // 16
    xhalf = x // 2
    xl_me = x % 2
    count = len_ref[g]
    mate = (g, x, yl * 2 + 1 - c)
    own = jnp.logical_and(xhalf == c, zp == c)

    def dest(i):
        dr = i % 16
        xl = (i // 16) % 2
        dyl = i // 32
        r = ((yh + dr // 8) % 2) * 8 + (z + dr) % 8
        y2 = (yl + dyl) % 2
        return r, xl, y2, (r, 2 * c + xl, y2 * 2 + zp)

    def is_self(i):
        return jnp.logical_and(own, i == xl_me * 16)

    def source(s):
        return (
            (s // 32) * 8 + ((s // 8) % 4) * 2 + c,
            (s // 2) % 4,
            (s % 2) * 2 + xhalf,
        )

    def remote(src, dst, ssem, rsem, to):
        return pltpu.make_async_remote_copy(
            src_ref=src, dst_ref=dst, send_sem=ssem, recv_sem=rsem,
            device_id=to, device_id_type=MESH,
        )

    barrier = pltpu.get_barrier_semaphore()

    def greet(i, carry):
        me_too = is_self(i)
        to = dest(i)[3]

        @pl.when(jnp.logical_not(me_too))
        def _():
            pl.semaphore_signal(barrier, inc=1, device_id=to, device_id_type=MESH)

        @pl.when(jnp.logical_not(jnp.logical_and(own, i == slot)))
        def _():
            pl.semaphore_signal(barrier, inc=1, device_id=source(i), device_id_type=MESH)

        return carry

    lax.fori_loop(0, SLOTS, greet, 0)
    pl.semaphore_signal(barrier, inc=1, device_id=mate, device_id_type=MESH)

    def norm_into(ref, gain_ref, at):
        def one(t, carry):
            wide = ref[t].astype(F32)
            power = jnp.mean(wide * wide, axis=-1, keepdims=True)
            y = (wide * lax.rsqrt(power + 1e-06) * gain_ref[...]).astype(BF)
            halves[0, at, t] = y[:, :HALF]
            halves[1, at, t] = y[:, HALF:]
            return carry

        lax.fori_loop(0, T, one, 0)

    def move_v(t, carry):
        halves[0, 2, t] = v_ref[t, :, :HALF]
        halves[1, 2, t] = v_ref[t, :, HALF:]
        return carry

    norm_into(q_ref, qg_ref, 0)
    norm_into(k_ref, kg_ref, 1)
    lax.fori_loop(0, T, move_v, 0)

    @pl.when(own)
    def _():
        pl.semaphore_wait(barrier, 2 * SLOTS - 1)

    @pl.when(jnp.logical_not(own))
    def _():
        pl.semaphore_wait(barrier, 2 * SLOTS + 1)

    exch = []
    for at in range(3):
        cp = remote(halves.at[1 - c, at], mates.at[at], ex_s.at[at], ex_r.at[at], mate)
        cp.start()
        exch.append(cp)

    shape = (R * 2 * T, R * 2 * T)
    orow = lax.broadcasted_iota(jnp.int32, (R, 2 * T, R * 2 * T), 0)
    ow = lax.broadcasted_iota(jnp.int32, (R, 2 * T, R * 2 * T), 1)
    occ = (ow >= T).astype(jnp.int32)
    want = (jnp.where(occ == c, 0, 1) * T + ow - T * occ) * R + orow
    col = lax.broadcasted_iota(jnp.int32, (R, 2 * T, R * 2 * T), 2)
    perm[...] = (want == col).astype(F32).reshape(shape).astype(BF)

    lane0 = (lax.broadcasted_iota(jnp.int32, (TILE, HD), 1) == 0).astype(F32).astype(BF)

    def live_rows(first, step, offset, zpar):
        s = (lax.broadcasted_iota(jnp.int32, (16, 2 * T, HD), 0) + first) * step + offset
        return (slot_pos((16, 2 * T, HD), s, zpar) < count).astype(F32).reshape(TILE, HD)

    def masks(i, carry):
        half = i // 4
        flag = live_rows((i % 4) * 16, 1, 0, jnp.where(half == 0, c, 1 - c))
        rows = pl.ds(pl.multiple_of(i * TILE, TILE), TILE)
        for h in range(3):
            ka[h, rows, HD:] = ((flag - 1.0) * 1e30).astype(BF)
            va[h, rows, HD:] = jnp.ones((TILE, HD), BF)
        return carry

    lax.fori_loop(0, 8, masks, 0)

    for at in range(3):
        exch[at].wait()

    def pack(at, xl, first, width):
        cols = slice(xl * 640 + first * HD, xl * 640 + (first + width) * HD)
        mine = halves[c, at, :, :, cols].reshape(T * R, width * HD)
        theirs = mates[at, :, :, cols].reshape(T * R, width * HD)
        both = jnp.concatenate([mine, theirs], axis=0)
        res = jnp.dot(perm[...], both, preferred_element_type=F32)
        return res.reshape(R, 2 * T, width * HD)

    for at in range(3):
        for xl in range(2):
            for y2 in range(2):
                res = pack(at, xl, 3 * y2, 2)
                two = jnp.concatenate([res[:, :, :HD], res[:, :, HD:]], axis=1)
                sb[:, xl, y2, at * 48 : at * 48 + 48, :] = two.astype(BF)

    def send_main(i, carry):
        r, xl, y2, to = dest(i)
        src = sb.at[r, xl, y2]
        dst = rb.at[slot]

        @pl.when(is_self(i))
        def _():
            pltpu.make_async_copy(src, dst, main_r.at[sgrp]).start()

        @pl.when(jnp.logical_not(is_self(i)))
        def _():
            remote(src, dst, main_s, main_r.at[sgrp], to).start()

        return carry

    lax.fori_loop(0, SLOTS, send_main, 0)

    for xl in range(2):
        kv = jnp.concatenate([pack(1, xl, 2, 1), pack(2, xl, 2, 1)], axis=1)
        ss[:, xl, 0:48, :] = kv.astype(BF)
        qq = jnp.concatenate([pack(0, xl, 2, 1), jnp.zeros((R, 8, HD), F32)], axis=1)
        ss[:, xl, 48:80, :] = qq.astype(BF)

    def send_shared(i, carry):
        r, xl, y2, to = dest(i)

        @pl.when(i < 32)
        def _():
            src = ss.at[r, xl]
            dst = rsh.at[slot // 2, yl]

            @pl.when(is_self(i))
            def _():
                pltpu.make_async_copy(src, dst, sh_same.at[sgrp]).start()

            @pl.when(jnp.logical_not(is_self(i)))
            def _():
                remote(src, dst, sh_s.at[0], sh_same.at[sgrp], to).start()

        @pl.when(i >= 32)
        def _():
            src = ss.at[r, xl, pl.ds(0, 48)]
            dst = rsh.at[slot // 2, yl, pl.ds(0, 48)]
            remote(src, dst, sh_s.at[1], sh_other.at[sgrp], to).start()

        return carry

    lax.fori_loop(0, SLOTS, send_shared, 0)

    def place(ref, h, rows, value):
        ref[h, rows, :HD] = value.reshape(TILE, HD).astype(BF)

    def wait_for(ref, sem):
        pltpu.make_async_copy(ref, ref, sem).wait()

    forwards = []
    for i in range(4):
        at = pl.ds(16 * i, 16)
        wait_for(rb.at[at], main_r.at[i])
        cp = remote(
            rb.at[at, pl.ds(48, 96)], rm.at[at], fwd_s.at[i], fwd_r.at[i], mate
        )
        cp.start()
        forwards.append(cp)
        kk = rb[16 * i : 16 * i + 16, 48:96, :].astype(F32)
        vv = rb[16 * i : 16 * i + 16, 96:144, :].astype(F32)
        rows = slice(i * TILE, (i + 1) * TILE)
        for h in range(2):
            place(ka, h, rows, kk[:, 24 * h : 24 * h + 24])
            place(va, h, rows, vv[:, 24 * h : 24 * h + 24])
    for i in range(4):
        forwards[i].wait()
        kk = rm[16 * i : 16 * i + 16, 0:48, :].astype(F32)
        vv = rm[16 * i : 16 * i + 16, 48:96, :].astype(F32)
        rows = slice((i + 4) * TILE, (i + 5) * TILE)
        for h in range(2):
            place(ka, h, rows, kk[:, 24 * h : 24 * h + 24])
            place(va, h, rows, vv[:, 24 * h : 24 * h + 24])

    scale = F32(HD ** (-0.5) * LOG2E)

    def attend(q, h, live):
        qa = jnp.concatenate([q, lane0], axis=1)
        top = None
        step = 512
        for j in range(KEYS // step):
            cols = slice(j * step, (j + 1) * step)
            part = lax.dot_general(
                qa, ka[h, cols, :], (((1,), (1,)), ((), ())),
                preferred_element_type=F32,
            )
            scr[:, cols] = part
            for i in range(step // HD):
                piece = part[:, i * HD : (i + 1) * HD]
                top = piece if top is None else jnp.maximum(top, piece)
        peak = jnp.max(top, axis=1, keepdims=True)
        for j in range(KEYS // step):
            cols = slice(j * step, (j + 1) * step)
            prb[:, cols] = jnp.exp2((scr[:, cols] - peak) * scale).astype(BF)
        mixed = jnp.dot(prb[...], va[h], preferred_element_type=F32)
        return jnp.where(live > 0.0, mixed[:, :HD] / mixed[:, HD:], 0.0)

    def main_tile(i, carry):
        at = pl.ds(pl.multiple_of(i * 16, 16), 16)
        live = live_rows(i * 16, 1, 0, c)
        qq = rb[at, 0:48, :].astype(F32)
        res = []
        for h in range(2):
            q = qq[:, 24 * h : 24 * h + 24].reshape(TILE, HD).astype(BF)
            res.append(attend(q, h, live).reshape(16, 2 * T, HD))
        obs[at] = jnp.concatenate(res, axis=1).astype(BF)

        def send(j, carry):
            s = i * 16 + j
            dst = ob.at[g, xl_me, yl]
            mine = jnp.logical_and(own, s == slot)

            @pl.when(mine)
            def _():
                pltpu.make_async_copy(obs.at[s], dst, o_r.at[xl_me]).start()

            @pl.when(jnp.logical_not(mine))
            def _():
                remote(obs.at[s], dst, o_s, o_r.at[xl_me], source(s)).start()

            return carry

        lax.fori_loop(0, 16, send, 0)
        return carry

    lax.fori_loop(0, 4, main_tile, 0)

    forwards = []
    for i in range(4):
        at = pl.ds(8 * i, 8)
        wait_for(rsh.at[at, yl], sh_same.at[i])
        wait_for(rsh.at[at, 1 - yl, pl.ds(0, 48)], sh_other.at[i])
        cp = remote(
            rsh.at[at, :, pl.ds(0, 48)], rmsh.at[at], fsh_s.at[i], fsh_r.at[i], mate
        )
        cp.start()
        forwards.append(cp)
        kv = rsh[8 * i : 8 * i + 8, :, 0:48, :].astype(F32).reshape(16, 48, HD)
        rows = slice(i * TILE, (i + 1) * TILE)
        place(ka, 2, rows, kv[:, 0:24])
        place(va, 2, rows, kv[:, 24:48])
    for i in range(4):
        forwards[i].wait()
        kv = rmsh[8 * i : 8 * i + 8].astype(F32).reshape(16, 48, HD)
        rows = slice((i + 4) * TILE, (i + 5) * TILE)
        place(ka, 2, rows, kv[:, 0:24])
        place(va, 2, rows, kv[:, 24:48])

    def shared_tile(i, carry):
        at = pl.ds(pl.multiple_of(i * 16, 16), 16)
        live = live_rows(i * 16, 2, yl, c)
        qq = rsh[at, yl, 48:80, :].astype(F32)
        q = qq[:, 0:24].reshape(TILE, HD).astype(BF)
        res = attend(q, 2, live).reshape(16, 2 * T, HD)
        oshs[at] = jnp.concatenate([res, jnp.zeros((16, 8, HD), F32)], axis=1).astype(BF)

        def send(j, carry):
            m = i * 16 + j
            s = m * 2 + yl
            dst = osh.at[g, xl_me]
            mine = jnp.logical_and(own, s == slot)

            @pl.when(mine)
            def _():
                pltpu.make_async_copy(oshs.at[m], dst, osh_r.at[xl_me]).start()

            @pl.when(jnp.logical_not(mine))
            def _():
                remote(oshs.at[m], dst, osh_s, osh_r.at[xl_me], source(s)).start()

            return carry

        lax.fori_loop(0, 16, send, 0)
        return carry

    lax.fori_loop(0, 2, shared_tile, 0)

    def unpack(value):
        res = lax.dot_general(
            perm[...], value, (((0,), (0,)), ((), ())), preferred_element_type=F32
        )
        return res.astype(BF)

    def store(res, xl, first, width):
        cols = slice(xl * 640 + first * HD, xl * 640 + (first + width) * HD)
        fin[0, :, :, cols] = res[: T * R].reshape(T, R, width * HD)
        fin[1, :, :, cols] = res[T * R :].reshape(T, R, width * HD)

    for xl in range(2):
        wait_for(ob.at[:, xl], o_r.at[xl])
        for y2 in range(2):
            got = ob[:, xl, y2].astype(F32)
            flat = [got[:, 24 * h : 24 * h + 24].reshape(TILE, HD) for h in range(2)]
            store(unpack(jnp.concatenate(flat, axis=1).astype(BF)), xl, 3 * y2, 2)
    for xl in range(2):
        wait_for(osh.at[:, xl], osh_r.at[xl])
        got = osh[:, xl].astype(F32)[:, 0:24].reshape(TILE, HD)
        store(unpack(got.astype(BF)), xl, 2, 1)

    cols = pl.ds(pl.multiple_of(c * HALF, HALF), HALF)
    far = remote(fin.at[1], out_ref.at[:, :, cols], fin_s, fin_r, mate)
    far.start()
    near = pltpu.make_async_copy(fin.at[0], out_ref.at[:, :, cols], fin_l)
    near.start()
    far.wait()
    near.wait()

    @pl.when(own)
    def _():
        wait_for(rb.at[pl.ds(0, SLOTS - 1)], main_s)
        wait_for(rsh.at[pl.ds(0, 31), 0], sh_s.at[0])
        wait_for(obs.at[pl.ds(0, SLOTS - 1)], o_s)
        wait_for(oshs.at[pl.ds(0, 31)], osh_s)

    @pl.when(jnp.logical_not(own))
    def _():
        wait_for(rb, main_s)
        wait_for(rsh.at[:, 0], sh_s.at[0])
        wait_for(obs, o_s)
        wait_for(oshs, osh_s)

    wait_for(rsh.at[:, 0, pl.ds(0, 48)], sh_s.at[1])


def per_device(q_in, k_in, v_in, q_gain, k_gain, lengths):
    vm = pl.BlockSpec(memory_space=pltpu.VMEM)
    dma = pltpu.SemaphoreType.DMA
    scratch = [
        pltpu.VMEM((2, 3, T, R, HALF), BF),
        pltpu.VMEM((3, T, R, HALF), BF),
        pltpu.VMEM((TILE, TILE), BF),
        pltpu.VMEM((R, 2, 2, 144, HD), BF),
        pltpu.VMEM((R, 2, 80, HD), BF),
        pltpu.VMEM((SLOTS, 144, HD), BF),
        pltpu.VMEM((SLOTS // 2, 2, 80, HD), BF),
        pltpu.VMEM((SLOTS, 96, HD), BF),
        pltpu.VMEM((SLOTS // 2, 2, 48, HD), BF),
        pltpu.VMEM((3, KEYS, 2 * HD), BF),
        pltpu.VMEM((3, KEYS, 2 * HD), BF),
        pltpu.VMEM((TILE, KEYS), F32),
        pltpu.VMEM((TILE, KEYS), BF),
        pltpu.VMEM((8, HD), F32),
        pltpu.VMEM((SLOTS, 48, HD), BF),
        pltpu.VMEM((SLOTS // 2, 32, HD), BF),
        pltpu.VMEM((R, 2, 2, 48, HD), BF),
        pltpu.VMEM((R, 2, 32, HD), BF),
        pltpu.VMEM((2, T, R, HALF), BF),
        dma((3,)), dma((3,)),
        dma, dma((4,)),
        dma((4,)), dma((4,)),
        dma((2,)), dma((4,)), dma((4,)),
        dma((4,)), dma((4,)),
        dma, dma((2,)),
        dma, dma((2,)),
        dma, dma, dma,
    ]
    res = pl.pallas_call(
        kernel,
        out_shape=jax.ShapeDtypeStruct((T, R, 2 * HALF), BF),
        in_specs=[pl.BlockSpec(memory_space=pltpu.SMEM), vm, vm, vm, vm, vm],
        out_specs=pl.BlockSpec(memory_space=pl.ANY),
        scratch_shapes=scratch,
        compiler_params=pltpu.CompilerParams(
            collective_id=0, has_side_effects=True, vmem_limit_bytes=60 << 20
        ),
        name="attend",
    )(
        lengths,
        jnp.transpose(q_in, (1, 0, 2)),
        jnp.transpose(k_in, (1, 0, 2)),
        jnp.transpose(v_in, (1, 0, 2)),
        q_gain[None, :],
        k_gain[None, :],
    )
    return jnp.transpose(res, (1, 0, 2))


def solution(mesh):
    placed = P(None, ("grp", "uly", "blk"), None)
    return jax.shard_map(
        per_device,
        mesh=mesh,
        in_specs=(placed, placed, placed, P(), P(), P()),
        out_specs=placed,
        check_vma=False,
    )
```

time: 504 us -> 127 us (0.25)
  the two profiles are of different devices: /device:TPU:32 before, /device:TPU:31 now
where the time goes in v1:
time: 127 us; the launch traced here: 126 us
  Pallas kernels  122 us (96%)
  local copies, waits for them, and re-layouts  4.14 us (3%)
    pallas_call x1, Pallas kernels, per_device(): pl.pallas_call(kernel, out_shape=jax.ShapeDtypeStruct((T, R, 2 * HALF), B...  122 us

profile of v1, /device:TPU:31, one launch (start us, length us, event | category | flops | bytes accessed | tf_op | source)
XLA Modules:
  0.0 126.3 jit_solution(4724702921618048945)
XLA Ops:
  0.0 0.0 copy-start
  0.0 1.3 %broadcast_in_dim.6.qg_ref = f32[1,2560]{1,0:T(1,128)} reshape(f32[2560]{0:T(1024)} %param.9) | data formatting | bytes 20480 | tf_op jit(solution)/shard_map/broadcast_in_dim | solution.py:456
  1.3 0.0 copy-done
  1.3 0.6 broadcast_in_dim.7.kg_ref
  1.9 122.2 %attend.1 = bf16[12,16,2560]{2,1,0:T(8,128)(2,1)} custom-call(s32[16]{0:T(128)} %len_ref.1, bf16[12,16,2560]{2,1,0:T(8,128)(2,1)} %bitcast.5, bf16[12,16,2560]{2,1,0:T(8,128)(2,1)} %bitcast.6, bf16[12,16,2560]{2,1,0:T(8,128)(2,1)} %bitcast.7, f32[1,2560]{1,0:T(1,128)} %broadcast_in_dim.6.qg_ref, f32[1,2560]{1,0:T(1,128)} %broadcast_in_dim.7.kg_ref), custom_call_target="tpu_custom_call" | custom-call | tf_op jit(solution)/shard_map/attend/pallas_call | solution.py:441
  124.1 2.2 %copy.8 = bf16[16,12,2560]{2,0,1:T(8,128)(2,1)} copy(bf16[16,12,2560]{2,0,1:T(8,128)(2,1)} %bitcast.4) | data formatting | bytes 1966080
Async XLA Ops:
  0.0 1.3 %copy-start = (f32[2560]{0:T(1024)S(1)}, f32[2560]{0:T(1024)}, u32[]{:S(2)}) copy-start(f32[2560]{0:T(1024)} %param.10) | copy-start | bytes 30724

commit v2 on v1

--- a/solution.py
+++ b/solution.py
@@ -35,9 +35,9 @@
 
 def kernel(
     len_ref, q_ref, k_ref, v_ref, qg_ref, kg_ref, out_ref,
-    halves, mates, perm, sb, ss, rb, rsh, rm, rmsh, ka, va, scr, prb, of,
+    halves, mates, perm, sb, ss, rb, rsh, rn, rm, rmsh, ka, va, scr, prb,
     obs, oshs, ob, osh, fin,
-    ex_s, ex_r, main_s, main_r, fwd_s, fwd_r, sh_s, sh_same, sh_other, fsh_s, fsh_r,
+    ex_s, ex_r, main_s, main_r, fwd_s, fwd_r, sh_s, sh_r, near_s, near_r, fsh_s, fsh_r,
     o_s, o_r, osh_s, osh_r, fin_s, fin_r, fin_l,
 ):
     g = lax.axis_index("grp")
@@ -55,6 +55,7 @@
     xl_me = x % 2
     count = len_ref[g]
     mate = (g, x, yl * 2 + 1 - c)
+    next_chip = (g, x, (1 - yl) * 2 + c)
     own = jnp.logical_and(xhalf == c, zp == c)
 
     def dest(i):
@@ -99,12 +100,13 @@
 
     lax.fori_loop(0, SLOTS, greet, 0)
     pl.semaphore_signal(barrier, inc=1, device_id=mate, device_id_type=MESH)
+    pl.semaphore_signal(barrier, inc=1, device_id=next_chip, device_id_type=MESH)
 
     def norm_into(ref, gain_ref, at):
         def one(t, carry):
             wide = ref[t].astype(F32)
             power = jnp.mean(wide * wide, axis=-1, keepdims=True)
-            y = (wide * lax.rsqrt(power + 1e-06) * gain_ref[...]).astype(BF)
+            y = (wide * lax.rsqrt(power + 1e-06) * gain_ref[...][None, :]).astype(BF)
             halves[0, at, t] = y[:, :HALF]
             halves[1, at, t] = y[:, HALF:]
             return carry
@@ -122,11 +124,11 @@
 
     @pl.when(own)
     def _():
-        pl.semaphore_wait(barrier, 2 * SLOTS - 1)
+        pl.semaphore_wait(barrier, 2 * SLOTS)
 
     @pl.when(jnp.logical_not(own))
     def _():
-        pl.semaphore_wait(barrier, 2 * SLOTS + 1)
+        pl.semaphore_wait(barrier, 2 * SLOTS + 2)
 
     exch = []
     for at in range(3):
@@ -152,9 +154,15 @@
         half = i // 4
         flag = live_rows((i % 4) * 16, 1, 0, jnp.where(half == 0, c, 1 - c))
         rows = pl.ds(pl.multiple_of(i * TILE, TILE), TILE)
-        for h in range(3):
+        for h in range(2):
             ka[h, rows, HD:] = ((flag - 1.0) * 1e30).astype(BF)
             va[h, rows, HD:] = jnp.ones((TILE, HD), BF)
+        side = (i // 2) % 2
+        flag = live_rows(
+            (i % 2) * 16, 2, jnp.where(side == 0, yl, 1 - yl), jnp.where(half == 0, c, 1 - c)
+        )
+        ka[2, rows, HD:] = ((flag - 1.0) * 1e30).astype(BF)
+        va[2, rows, HD:] = jnp.ones((TILE, HD), BF)
         return carry
 
     lax.fori_loop(0, 8, masks, 0)
@@ -202,29 +210,20 @@
 
     def send_shared(i, carry):
         r, xl, y2, to = dest(i)
-
-        @pl.when(i < 32)
-        def _():
-            src = ss.at[r, xl]
-            dst = rsh.at[slot // 2, yl]
-
-            @pl.when(is_self(i))
-            def _():
-                pltpu.make_async_copy(src, dst, sh_same.at[sgrp]).start()
-
-            @pl.when(jnp.logical_not(is_self(i)))
-            def _():
-                remote(src, dst, sh_s.at[0], sh_same.at[sgrp], to).start()
-
-        @pl.when(i >= 32)
-        def _():
-            src = ss.at[r, xl, pl.ds(0, 48)]
-            dst = rsh.at[slot // 2, yl, pl.ds(0, 48)]
-            remote(src, dst, sh_s.at[1], sh_other.at[sgrp], to).start()
-
-        return carry
-
-    lax.fori_loop(0, SLOTS, send_shared, 0)
+        src = ss.at[r, xl]
+        dst = rsh.at[slot // 2]
+
+        @pl.when(is_self(i))
+        def _():
+            pltpu.make_async_copy(src, dst, sh_r.at[yh]).start()
+
+        @pl.when(jnp.logical_not(is_self(i)))
+        def _():
+            remote(src, dst, sh_s, sh_r.at[yh], to).start()
+
+        return carry
+
+    lax.fori_loop(0, SLOTS // 2, send_shared, 0)
 
     def place(ref, h, rows, value):
         ref[h, rows, :HD] = value.reshape(TILE, HD).astype(BF)
@@ -309,31 +308,38 @@
 
     lax.fori_loop(0, 4, main_tile, 0)
 
-    forwards = []
-    for i in range(4):
-        at = pl.ds(8 * i, 8)
-        wait_for(rsh.at[at, yl], sh_same.at[i])
-        wait_for(rsh.at[at, 1 - yl, pl.ds(0, 48)], sh_other.at[i])
-        cp = remote(
-            rsh.at[at, :, pl.ds(0, 48)], rmsh.at[at], fsh_s.at[i], fsh_r.at[i], mate
-        )
-        cp.start()
-        forwards.append(cp)
-        kv = rsh[8 * i : 8 * i + 8, :, 0:48, :].astype(F32).reshape(16, 48, HD)
+    def place_shared(i, value):
+        kv = value.astype(F32)
         rows = slice(i * TILE, (i + 1) * TILE)
         place(ka, 2, rows, kv[:, 0:24])
         place(va, 2, rows, kv[:, 24:48])
+
+    across, along = [], []
+    for i in range(2):
+        at = pl.ds(16 * i, 16)
+        part = rsh.at[at, pl.ds(0, 48)]
+        wait_for(rsh.at[at], sh_r.at[i])
+        across.append(remote(part, rn.at[at], near_s.at[i], near_r.at[i], next_chip))
+        across[i].start()
+        along.append(remote(part, rmsh.at[0, at], fsh_s.at[i], fsh_r.at[i], mate))
+        along[i].start()
+        place_shared(i, rsh[16 * i : 16 * i + 16, 0:48, :])
+    for i in range(2):
+        at = pl.ds(16 * i, 16)
+        across[i].wait()
+        along.append(
+            remote(rn.at[at], rmsh.at[1, at], fsh_s.at[2 + i], fsh_r.at[2 + i], mate)
+        )
+        along[2 + i].start()
+        place_shared(2 + i, rn[16 * i : 16 * i + 16])
     for i in range(4):
-        forwards[i].wait()
-        kv = rmsh[8 * i : 8 * i + 8].astype(F32).reshape(16, 48, HD)
-        rows = slice((i + 4) * TILE, (i + 5) * TILE)
-        place(ka, 2, rows, kv[:, 0:24])
-        place(va, 2, rows, kv[:, 24:48])
+        along[i].wait()
+        place_shared(4 + i, rmsh[i // 2, 16 * (i % 2) : 16 * (i % 2) + 16])
 
     def shared_tile(i, carry):
         at = pl.ds(pl.multiple_of(i * 16, 16), 16)
         live = live_rows(i * 16, 2, yl, c)
-        qq = rsh[at, yl, 48:80, :].astype(F32)
+        qq = rsh[at, 48:80, :].astype(F32)
         q = qq[:, 0:24].reshape(TILE, HD).astype(BF)
         res = attend(q, 2, live).reshape(16, 2 * T, HD)
         oshs[at] = jnp.concatenate([res, jnp.zeros((16, 8, HD), F32)], axis=1).astype(BF)
@@ -392,18 +398,16 @@
     @pl.when(own)
     def _():
         wait_for(rb.at[pl.ds(0, SLOTS - 1)], main_s)
-        wait_for(rsh.at[pl.ds(0, 31), 0], sh_s.at[0])
+        wait_for(rsh.at[pl.ds(0, 31)], sh_s)
         wait_for(obs.at[pl.ds(0, SLOTS - 1)], o_s)
         wait_for(oshs.at[pl.ds(0, 31)], osh_s)
 
     @pl.when(jnp.logical_not(own))
     def _():
         wait_for(rb, main_s)
-        wait_for(rsh.at[:, 0], sh_s.at[0])
+        wait_for(rsh, sh_s)
         wait_for(obs, o_s)
         wait_for(oshs, osh_s)
-
-    wait_for(rsh.at[:, 0, pl.ds(0, 48)], sh_s.at[1])
 
 
 def per_device(q_in, k_in, v_in, q_gain, k_gain, lengths):
@@ -416,14 +420,14 @@
         pltpu.VMEM((R, 2, 2, 144, HD), BF),
         pltpu.VMEM((R, 2, 80, HD), BF),
         pltpu.VMEM((SLOTS, 144, HD), BF),
-        pltpu.VMEM((SLOTS // 2, 2, 80, HD), BF),
+        pltpu.VMEM((SLOTS // 2, 80, HD), BF),
+        pltpu.VMEM((SLOTS // 2, 48, HD), BF),
         pltpu.VMEM((SLOTS, 96, HD), BF),
-        pltpu.VMEM((SLOTS // 2, 2, 48, HD), BF),
+        pltpu.VMEM((2, SLOTS // 2, 48, HD), BF),
         pltpu.VMEM((3, KEYS, 2 * HD), BF),
         pltpu.VMEM((3, KEYS, 2 * HD), BF),
         pltpu.VMEM((TILE, KEYS), F32),
         pltpu.VMEM((TILE, KEYS), BF),
-        pltpu.VMEM((8, HD), F32),
         pltpu.VMEM((SLOTS, 48, HD), BF),
         pltpu.VMEM((SLOTS // 2, 32, HD), BF),
         pltpu.VMEM((R, 2, 2, 48, HD), BF),
@@ -432,7 +436,8 @@
         dma((3,)), dma((3,)),
         dma, dma((4,)),
         dma((4,)), dma((4,)),
-        dma((2,)), dma((4,)), dma((4,)),
+        dma, dma((2,)),
+        dma((2,)), dma((2,)),
         dma((4,)), dma((4,)),
         dma, dma((2,)),
         dma, dma((2,)),
@@ -453,8 +458,8 @@
         jnp.transpose(q_in, (1, 0, 2)),
         jnp.transpose(k_in, (1, 0, 2)),
         jnp.transpose(v_in, (1, 0, 2)),
-        q_gain[None, :],
-        k_gain[None, :],
+        q_gain,
+        k_gain,
     )
     return jnp.transpose(res, (1, 0, 2))
 

time: 127 us -> 133 us (1.047)
  Pallas kernels: 122 us -> 130 us
  local copies, waits for them, and re-layouts: 4.14 us -> 2.21 us
    pallas_call x1, Pallas kernels: 122 us -> 130 us  [per_device(): pl.pallas_call(kernel, out_shape=jax.ShapeDtypeStruct((T, R, 2 * HALF), B...]
    broadcast_in_dim x2 -> x0, local copies, waits for them, and re-layouts: 1.93 us -> none  [the longest x1 1.33 us: per_device(): q_gain[None, :]]
where the time goes in v2:
time: 133 us
  Pallas kernels  130 us (98%)
  local copies, waits for them, and re-layouts  2.21 us (2%)
    pallas_call x1, Pallas kernels, per_device(): pl.pallas_call(kernel, out_shape=jax.ShapeDtypeStruct((T, R, 2 * HALF), B...  130 us

profile of v2, /device:TPU:31, one launch (start us, length us, event | category | flops | bytes accessed | tf_op | source)
XLA Modules:
  0.0 132.6 jit_solution(16941968223153928907)
XLA Ops:
  0.0 130.4 %attend.1 = bf16[12,16,2560]{2,1,0:T(8,128)(2,1)} custom-call(s32[16]{0:T(128)} %len_ref.1, bf16[12,16,2560]{2,1,0:T(8,128)(2,1)} %bitcast.5, bf16[12,16,2560]{2,1,0:T(8,128)(2,1)} %bitcast.6, bf16[12,16,2560]{2,1,0:T(8,128)(2,1)} %bitcast.7, f32[2560]{0:T(1024)} %qg_ref.1, f32[2560]{0:T(1024)} %kg_ref.1), custom_call_target="tpu_custom_call" | custom-call | tf_op jit(solution)/shard_map/attend/pallas_call | solution.py:446
  130.4 2.2 %copy.8 = bf16[16,12,2560]{2,0,1:T(8,128)(2,1)} copy(bf16[16,12,2560]{2,0,1:T(8,128)(2,1)} %bitcast.4) | data formatting | bytes 1966080

commit v3 on v2

v3 whole, which is shorter than its diff:
```python
import functools
import math

import jax
import jax.numpy as jnp
from jax import lax
from jax.experimental import pallas as pl
from jax.experimental.pallas import tpu as pltpu
from jax.sharding import PartitionSpec as P

HD = 128
T = 12
R = 16
HALF = 1280
SLOTS = 64
KEYS = 3072
TILE = 384
BLOCK = 768
SUB = 256
REACH = 1536
CUT = 12
LOG2E = math.log2(math.e)
MESH = pl.DeviceIdType.MESH
BF = jnp.bfloat16
F32 = jnp.float32


def slot_pos(shape, slot, zpar):
    w = lax.broadcasted_iota(jnp.int32, shape, 1)
    cc = (w >= T).astype(jnp.int32)
    t = w - T * cc
    x = slot & 3
    zh = (slot >> 2) & 3
    yh = (slot >> 4) & 1
    yl = slot >> 5
    z = zh * 2 + zpar
    return ((((yl * 2 + cc) * 4 + x) * 2 + yh) * 8 + z) * T + t


def group_rank(yh, z):
    k = (z >> 1) + 4 * (z & 1)
    return jnp.where((k & 1) == yh, k, 15 - k)


def rank_group(k):
    j = k if k < 8 else 15 - k
    z = 2 * (j & 3) + (j >> 2)
    yh = (j & 1) if k < 8 else 1 - (j & 1)
    return yh * 8 + z


def kernel(
    cut,
    len_ref, q_ref, k_ref, v_ref, qg_ref, kg_ref, out_ref,
    halves, mates, perm, sb, ss, rel, rels, rb, rsh, rm, rmsh, ka, va, scr,
    obs, oshs, ob, osh, fin,
    ex_s, ex_r, main_s, main_r, fwd_s, fwd_r, sh_s, sh_r, fsh_s, fsh_r,
    rel_s, rel_r, rels_s, rels_r, o_s, o_r, osh_s, osh_r, fin_s, fin_r, fin_l,
):
    g = lax.axis_index("grp")
    x = lax.axis_index("uly")
    blk = lax.axis_index("blk")
    c = blk & 1
    yl = blk >> 1
    z = g & 7
    yh = g >> 3
    zp = z & 1
    zh = z >> 1
    slot = ((yl * 2 + yh) * 4 + zh) * 4 + x
    sgrp = slot >> 4
    xhalf = x >> 1
    xl_me = x & 1
    rank_me = group_rank(yh, z)
    short = rank_me >= cut
    three = yl == (zp ^ xl_me)
    mate = (g, x, yl * 2 + 1 - c)
    next_chip = (g, x, (1 - yl) * 2 + c)
    own = jnp.logical_and(xhalf == c, zp == c)

    def dest(i):
        dr = i & 15
        xl = (i >> 4) & 1
        ty = yh ^ (dr >> 3)
        tz = (z + dr) & 7
        y2 = yl ^ (i >> 5)
        return group_rank(ty, tz), xl, y2, ((ty << 3) | tz, 2 * c + xl, y2 * 2 + zp)

    def is_self(i):
        return jnp.logical_and(own, i == xl_me * 16)

    def source(s):
        return (
            (((s >> 4) & 1) << 3) | (((s >> 2) & 3) << 1) | c,
            s & 3,
            ((s >> 5) << 1) | xhalf,
        )

    def remote(src, dst, ssem, rsem, to):
        return pltpu.make_async_remote_copy(
            src_ref=src, dst_ref=dst, send_sem=ssem, recv_sem=rsem,
            device_id=to, device_id_type=MESH,
        )

    def send(src, dst, ssem, rsem, to, here):
        @pl.when(here)
        def _():
            pltpu.make_async_copy(src, dst, rsem).start()

        @pl.when(jnp.logical_not(here))
        def _():
            remote(src, dst, ssem, rsem, to).start()

    def wait_for(ref, sem):
        pltpu.make_async_copy(ref, ref, sem).wait()

    barrier = pltpu.get_barrier_semaphore()

    def greet(i, carry):
        @pl.when(jnp.logical_not(is_self(i)))
        def _():
            pl.semaphore_signal(barrier, inc=1, device_id=dest(i)[3], device_id_type=MESH)

        @pl.when(jnp.logical_not(jnp.logical_and(own, i == slot)))
        def _():
            pl.semaphore_signal(barrier, inc=1, device_id=source(i), device_id_type=MESH)

        return carry

    lax.fori_loop(0, SLOTS, greet, 0)
    pl.semaphore_signal(barrier, inc=1, device_id=mate, device_id_type=MESH)
    pl.semaphore_signal(barrier, inc=1, device_id=next_chip, device_id_type=MESH)

    sizes = [len_ref[i] for i in range(R)]
    ranks = []
    count = jnp.int32(0)
    for i in range(R):
        rank = jnp.int32(0)
        for j in range(R):
            if j != i:
                ahead = sizes[j] >= sizes[i] if j < i else sizes[j] > sizes[i]
                rank = rank + ahead.astype(jnp.int32)
        ranks.append(rank)
        count = count + jnp.where(rank == rank_me, sizes[i], 0)

    def norm_into(ref, gain_ref, at):
        def one(t, carry):
            wide = ref[t].astype(F32)
            power = jnp.mean(wide * wide, axis=-1, keepdims=True)
            y = (wide * lax.rsqrt(power + 1e-06) * gain_ref[...][None, :]).astype(BF)
            halves[0, at, t] = y[:, :HALF]
            halves[1, at, t] = y[:, HALF:]
            return carry

        lax.fori_loop(0, T, one, 0)

    def move_v(t, carry):
        halves[0, 2, t] = v_ref[t, :, :HALF]
        halves[1, 2, t] = v_ref[t, :, HALF:]
        return carry

    norm_into(q_ref, qg_ref, 0)
    norm_into(k_ref, kg_ref, 1)
    lax.fori_loop(0, T, move_v, 0)

    @pl.when(own)
    def _():
        pl.semaphore_wait(barrier, 2 * SLOTS)

    @pl.when(jnp.logical_not(own))
    def _():
        pl.semaphore_wait(barrier, 2 * SLOTS + 2)

    exch = []
    for at in range(3):
        cp = remote(halves.at[1 - c, at], mates.at[at], ex_s.at[at], ex_r.at[at], mate)
        cp.start()
        exch.append(cp)

    shape = (R, 2 * T, TILE)
    ow = lax.broadcasted_iota(jnp.int32, shape, 1)
    occ = (ow >= T).astype(jnp.int32)
    col = lax.broadcasted_iota(jnp.int32, (1, 1, TILE), 2)
    rank_of = jnp.zeros((1, 1, TILE), jnp.int32)
    for i in range(R):
        rank_of = jnp.where((col & 15) == i, ranks[i], rank_of)
    place_of = (col >> 4) + 64 * rank_of
    want = jnp.where(occ == c, 0, 1) * T + ow - T * occ
    want = want + 64 * lax.broadcasted_iota(jnp.int32, shape, 0)
    perm[...] = (want == place_of).astype(F32).reshape(TILE, TILE).astype(BF)

    lane0 = (lax.broadcasted_iota(jnp.int32, (SUB, HD), 1) == 0).astype(F32).astype(BF)

    def live_rows(slots, first, zpar):
        s = lax.broadcasted_iota(jnp.int32, (slots, 2 * T, HD), 0) + first
        flag = slot_pos((slots, 2 * T, HD), s, zpar) < count
        return flag.astype(F32).reshape(slots * 2 * T, HD)

    def masks(i, carry):
        flag = live_rows(16, (i & 3) * 16, jnp.where(i < 4, c, 1 - c))
        rows = pl.ds(pl.multiple_of(i * TILE, TILE), TILE)
        for h in range(3):
            ka[h, rows, HD:] = ((flag - 1.0) * 1e30).astype(BF)
            va[h, rows, HD:] = jnp.ones((TILE, HD), BF)
        return carry

    lax.fori_loop(0, 8, masks, 0)

    for at in range(3):
        exch[at].wait()

    def pack(at, xl, first, width):
        cols = slice(xl * 640 + first * HD, xl * 640 + (first + width) * HD)
        mine = halves[c, at, :, :, cols].reshape(T * R, width * HD)
        theirs = mates[at, :, :, cols].reshape(T * R, width * HD)
        both = jnp.concatenate([mine, theirs], axis=0)
        res = jnp.dot(perm[...], both, preferred_element_type=F32)
        return res.reshape(R, 2 * T, width * HD)

    parts = ((0, 4, 0), (4, 12, 1), (12, 16, 0))

    for at in range(3):
        for xl in range(2):
            for hp in range(2):
                res = pack(at, xl, 3 * hp, 2)
                two = jnp.concatenate([res[:, :, :HD], res[:, :, HD:]], axis=1).astype(BF)
                for lo, hi, odd in parts:
                    sb[lo:hi, xl, hp ^ odd ^ xl, at * 48 : at * 48 + 48, :] = two[lo:hi]

    far_ranks = R - cut
    if far_ranks:
        @pl.when(yl == 0)
        def _():
            remote(sb.at[pl.ds(cut, far_ranks), :, 1], rel, rel_s, rel_r, next_chip).start()

    def send_main(i, carry):
        k, xl, y2, to = dest(i)
        ok = jnp.logical_or(k < cut, jnp.logical_and(yl == 0, y2 == 0))

        @pl.when(ok)
        def _():
            send(sb.at[k, xl, y2], rb.at[slot], main_s, main_r.at[sgrp], to, is_self(i))

        return carry

    lax.fori_loop(0, SLOTS, send_main, 0)

    for xl in range(2):
        kv = jnp.concatenate([pack(1, xl, 2, 1), pack(2, xl, 2, 1)], axis=1)
        ss[:, xl, 0:48, :] = kv.astype(BF)
        qq = jnp.concatenate([pack(0, xl, 2, 1), jnp.zeros((R, 8, HD), F32)], axis=1)
        ss[:, xl, 48:80, :] = qq.astype(BF)

    def pass_on(k, xl, src, dst, ssem, rsem):
        gk = rank_group(k)
        here = jnp.logical_and(own, jnp.logical_and(g == gk, xl_me == xl))
        send(src, dst, ssem, rsem, (gk, 2 * c + xl, 2 + zp), here)

    def spare(k):
        return 1 ^ (rank_group(k) & 1)

    if far_ranks:
        @pl.when(yl == 0)
        def _():
            for k in range(cut, R):
                at = k - cut
                remote(
                    ss.at[k, spare(k)], rels.at[at], rels_s.at[at], rels_r.at[at], next_chip
                ).start()

        @pl.when(yl == 1)
        def _():
            wait_for(rel, rel_r)
            for k in range(cut, R):
                for xl in range(2):
                    pass_on(
                        k, xl, rel.at[k - cut, xl], rb.at[slot & 31], main_s, main_r.at[yh]
                    )

    def send_shared(i, carry):
        dr = i & 15
        xl = i >> 4
        ty = yh ^ (dr >> 3)
        tz = (z + dr) & 7
        k = group_rank(ty, tz)
        y2 = (tz & 1) ^ xl
        ok = jnp.logical_or(k < cut, jnp.logical_and(yl == 0, y2 == 0))
        here = jnp.logical_and(is_self(i), three)

        @pl.when(ok)
        def _():
            send(
                ss.at[k, xl], rsh.at[slot], sh_s, sh_r.at[sgrp],
                ((ty << 3) | tz, 2 * c + xl, y2 * 2 + zp), here,
            )

        return carry

    lax.fori_loop(0, SLOTS // 2, send_shared, 0)

    if far_ranks:
        @pl.when(yl == 1)
        def _():
            for k in range(cut, R):
                at = k - cut
                wait_for(rels.at[at], rels_r.at[at])
                pass_on(k, spare(k), rels.at[at], rsh.at[slot & 31], sh_s, sh_r.at[yh])

    def place(ref, h, rows, value):
        ref[h, rows, :HD] = value.reshape(TILE, HD).astype(BF)

    def gather(some, arrived, forward, ours, theirs, heads):
        def lay(i, value):
            rows = slice(i * TILE, (i + 1) * TILE)
            kv = value.astype(F32)
            for n, h in enumerate(heads):
                place(ka, h, rows, kv[:, 24 * n : 24 * n + 24])
                m = n + len(heads)
                place(va, h, rows, kv[:, 24 * m : 24 * m + 24])

        def blank(i):
            rows = slice(i * TILE, (i + 1) * TILE)
            for h in heads:
                ka[h, rows, :HD] = jnp.zeros((TILE, HD), BF)
                va[h, rows, :HD] = jnp.zeros((TILE, HD), BF)

        def first(i):
            arrived(i)
            forward(i).start()
            lay(i, ours(i))

        def second(i):
            forward(i).wait()
            lay(4 + i, theirs(i))

        for step, shift in ((first, 0), (second, 4)):
            for i in range(4):
                if i < 2 or not some:
                    step(i)
                else:
                    @pl.when(short)
                    def _(i=i, shift=shift):
                        blank(shift + i)

                    @pl.when(jnp.logical_not(short))
                    def _(i=i, step=step):
                        step(i)

    def grp(i):
        return pl.ds(16 * i, 16)

    gather(
        far_ranks,
        lambda i: wait_for(rb.at[grp(i)], main_r.at[i]),
        lambda i: remote(
            rb.at[grp(i), pl.ds(48, 96)], rm.at[grp(i)], fwd_s.at[i], fwd_r.at[i], mate
        ),
        lambda i: rb[16 * i : 16 * i + 16, 48:144, :],
        lambda i: rm[16 * i : 16 * i + 16],
        (0, 1),
    )

    scale = HD ** (-0.5) * LOG2E

    def attend(q, h, live):
        step = 512
        outs = []
        for n in range(BLOCK // SUB):
            rows = slice(n * SUB, (n + 1) * SUB)
            qa = jnp.concatenate([q[rows], lane0], axis=1)
            top = None
            for j in range(KEYS // step):
                cols = slice(j * step, (j + 1) * step)
                part = lax.dot_general(
                    qa, ka[h, cols, :], (((1,), (1,)), ((), ())),
                    preferred_element_type=F32,
                )
                scr[rows, cols] = part
                for i in range(step // HD):
                    piece = part[:, i * HD : (i + 1) * HD]
                    top = piece if top is None else jnp.maximum(top, piece)
            peak = jnp.max(top, axis=1, keepdims=True)
            mixed = None
            for j in range(KEYS // step):
                cols = slice(j * step, (j + 1) * step)
                weights = jnp.exp2((scr[rows, cols] - peak) * scale).astype(BF)
                part = jnp.dot(weights, va[h, cols, :], preferred_element_type=F32)
                mixed = part if mixed is None else mixed + part
            outs.append(jnp.where(live[rows] > 0.0, mixed[:, :HD] / mixed[:, HD:], 0.0))
        return jnp.concatenate(outs, axis=0)

    passes = jnp.where(short, 1, 2)

    def back_from(ref, to, ssem, rsem, first):
        def back(j, carry):
            s = first + j
            here = jnp.logical_and(own, s == slot)
            send(ref.at[s], to, ssem, rsem, source(s), here)
            return carry

        lax.fori_loop(0, 32, back, 0)

    def main_pass(i, carry):
        at = pl.ds(pl.multiple_of(i * 32, 32), 32)
        live = live_rows(32, i * 32, c)
        qq = rb[at, 0:48, :].astype(F32)
        res = []
        for h in range(2):
            q = qq[:, 24 * h : 24 * h + 24].reshape(BLOCK, HD).astype(BF)
            res.append(attend(q, h, live).reshape(32, 2 * T, HD))
        obs[at] = jnp.concatenate(res, axis=1).astype(BF)
        rsem = o_r.at[xl_me, short.astype(jnp.int32)]
        back_from(obs, ob.at[rank_me, xl_me, yl], o_s, rsem, i * 32)
        return carry

    lax.fori_loop(0, passes, main_pass, 0)

    def third_pass(i, carry):
        at = pl.ds(pl.multiple_of(i * 32, 32), 32)
        live = live_rows(32, i * 32, c)
        q = rsh[at, 48:80, :].astype(F32)[:, 0:24].reshape(BLOCK, HD).astype(BF)
        res = attend(q, 2, live).reshape(32, 2 * T, HD)
        oshs[at] = jnp.concatenate([res, jnp.zeros((32, 8, HD), F32)], axis=1).astype(BF)
        rsem = osh_r.at[xl_me, short.astype(jnp.int32)]
        back_from(oshs, osh.at[rank_me, xl_me], osh_s, rsem, i * 32)
        return carry

    def sent_back(ref, sem):
        whole = jnp.logical_not(short)
        one = jnp.logical_and(own, jnp.logical_or(whole, yl == 0))
        for n, kind in ((SLOTS, whole), (SLOTS // 2, short)):
            if n == SLOTS or far_ranks:
                @pl.when(jnp.logical_and(kind, one))
                def _(n=n):
                    wait_for(ref.at[pl.ds(0, n - 1)], sem)

                @pl.when(jnp.logical_and(kind, jnp.logical_not(one)))
                def _(n=n):
                    wait_for(ref.at[pl.ds(0, n)], sem)

    @pl.when(three)
    def _():
        gather(
            far_ranks,
            lambda i: wait_for(rsh.at[grp(i)], sh_r.at[i]),
            lambda i: remote(
                rsh.at[grp(i), pl.ds(0, 48)], rmsh.at[grp(i)], fsh_s.at[i], fsh_r.at[i], mate
            ),
            lambda i: rsh[16 * i : 16 * i + 16, 0:48, :],
            lambda i: rmsh[16 * i : 16 * i + 16],
            (2,),
        )
        lax.fori_loop(0, passes, third_pass, 0)
        sent_back(oshs, osh_s)

    sent_back(obs, o_s)
    n_main = SLOTS - 2 * far_ranks
    n_shared = SLOTS // 2 - far_ranks

    def sent(ref, n, sem, one):
        @pl.when(one)
        def _():
            wait_for(ref.at[pl.ds(0, n - 1)], sem)

        @pl.when(jnp.logical_not(one))
        def _():
            wait_for(ref.at[pl.ds(0, n)], sem)

    sent(rb, n_main, main_s, own)
    sent(rsh, n_shared, sh_s, jnp.logical_and(own, three))
    if far_ranks:
        @pl.when(yl == 0)
        def _():
            wait_for(rel, rel_s)
            for at in range(far_ranks):
                wait_for(rels.at[at], rels_s.at[at])

    def unpack(value):
        res = lax.dot_general(
            perm[...], value, (((0,), (0,)), ((), ())), preferred_element_type=F32
        )
        return res.astype(BF)

    def store(res, xl, first, width):
        cols = slice(xl * 640 + first * HD, xl * 640 + (first + width) * HD)
        fin[0, :, :, cols] = res[: T * R].reshape(T, R, width * HD)
        fin[1, :, :, cols] = res[T * R :].reshape(T, R, width * HD)

    def returned(ref, sem, xl):
        wait_for(ref.at[pl.ds(0, cut), xl], sem.at[xl, 0])
        if far_ranks:
            @pl.when(yl == 0)
            def _():
                wait_for(ref.at[pl.ds(cut, far_ranks), xl], sem.at[xl, 1])

            @pl.when(yl == 1)
            def _():
                ref[cut:, xl] = jnp.zeros(ref[cut:, xl].shape, BF)

    for xl in range(2):
        returned(ob, o_r, xl)
        for hp in range(2):
            got = jnp.concatenate(
                [ob[lo:hi, xl, hp ^ odd ^ xl] for lo, hi, odd in parts], axis=0
            ).astype(F32)
            flat = [got[:, 24 * h : 24 * h + 24].reshape(TILE, HD) for h in range(2)]
            store(unpack(jnp.concatenate(flat, axis=1).astype(BF)), xl, 3 * hp, 2)
    for xl in range(2):
        returned(osh, osh_r, xl)
        got = osh[:, xl].astype(F32)[:, 0:24].reshape(TILE, HD)
        store(unpack(got.astype(BF)), xl, 2, 1)

    cols = pl.ds(pl.multiple_of(c * HALF, HALF), HALF)
    far = remote(fin.at[1], out_ref.at[:, :, cols], fin_s, fin_r, mate)
    far.start()
    near = pltpu.make_async_copy(fin.at[0], out_ref.at[:, :, cols], fin_l)
    near.start()
    far.wait()
    near.wait()


def run(cut, lengths, q, k, v, q_gain, k_gain):
    vm = pl.BlockSpec(memory_space=pltpu.VMEM)
    dma = pltpu.SemaphoreType.DMA
    far = max(R - cut, 1)
    scratch = [
        pltpu.VMEM((2, 3, T, R, HALF), BF),
        pltpu.VMEM((3, T, R, HALF), BF),
        pltpu.VMEM((TILE, TILE), BF),
        pltpu.VMEM((R, 2, 2, 144, HD), BF),
        pltpu.VMEM((R, 2, 80, HD), BF),
        pltpu.VMEM((far, 2, 144, HD), BF),
        pltpu.VMEM((far, 80, HD), BF),
        pltpu.VMEM((SLOTS, 144, HD), BF),
        pltpu.VMEM((SLOTS, 80, HD), BF),
        pltpu.VMEM((SLOTS, 96, HD), BF),
        pltpu.VMEM((SLOTS, 48, HD), BF),
        pltpu.VMEM((3, KEYS, 2 * HD), BF),
        pltpu.VMEM((3, KEYS, 2 * HD), BF),
        pltpu.VMEM((BLOCK, KEYS), F32),
        pltpu.VMEM((SLOTS, 48, HD), BF),
        pltpu.VMEM((SLOTS, 32, HD), BF),
        pltpu.VMEM((R, 2, 2, 48, HD), BF),
        pltpu.VMEM((R, 2, 32, HD), BF),
        pltpu.VMEM((2, T, R, HALF), BF),
        dma((3,)), dma((3,)),
        dma, dma((4,)),
        dma((4,)), dma((4,)),
        dma, dma((4,)),
        dma((4,)), dma((4,)),
        dma, dma, dma((far,)), dma((far,)),
        dma, dma((2, 2)),
        dma, dma((2, 2)),
        dma, dma, dma,
    ]
    return pl.pallas_call(
        functools.partial(kernel, cut),
        out_shape=jax.ShapeDtypeStruct((T, R, 2 * HALF), BF),
        in_specs=[pl.BlockSpec(memory_space=pltpu.SMEM), vm, vm, vm, vm, vm],
        out_specs=pl.BlockSpec(memory_space=pl.ANY),
        scratch_shapes=scratch,
        compiler_params=pltpu.CompilerParams(
            collective_id=cut, has_side_effects=True, vmem_limit_bytes=60 << 20
        ),
        name="attend_%d" % cut,
    )(lengths, q, k, v, q_gain, k_gain)


def per_device(q_in, k_in, v_in, q_gain, k_gain, lengths):
    args = (
        lengths,
        jnp.transpose(q_in, (1, 0, 2)),
        jnp.transpose(k_in, (1, 0, 2)),
        jnp.transpose(v_in, (1, 0, 2)),
        q_gain,
        k_gain,
    )
    fits = jnp.sum((lengths > REACH).astype(jnp.int32)) <= CUT
    res = lax.cond(
        fits,
        functools.partial(run, CUT),
        functools.partial(run, R),
        *args,
    )
    return jnp.transpose(res, (1, 0, 2))


def solution(mesh):
    placed = P(None, ("grp", "uly", "blk"), None)
    return jax.shard_map(
        per_device,
        mesh=mesh,
        in_specs=(placed, placed, placed, P(), P(), P()),
        out_specs=placed,
        check_vma=False,
    )
```

time: 133 us -> 119 us (0.89)
  Pallas kernels: 130 us -> 115 us
    pallas_call x1, Pallas kernels: 130 us -> 115 us  [run(): pl.pallas_call(functools.partial(kernel, cut), out_shape=jax.ShapeDtypeSt...]
where the time goes in v3:
time: 119 us
  Pallas kernels  115 us (97%)
  local copies, waits for them, and re-layouts  1.6 us (1%)
  other arithmetic  1.29 us (1%)
    pallas_call x1, Pallas kernels, run(): pl.pallas_call(functools.partial(kernel, cut), out_shape=jax.ShapeDtypeSt...  115 us

profile of v3, /device:TPU:31, one launch (start us, length us, event | category | flops | bytes accessed | tf_op | source)
XLA Modules:
  0.0 119.0 jit_solution(11055085149506573445)
XLA Ops:
  0.0 1.3 %fusion = s32[]{:T(128)} fusion(s32[16]{0:T(128)} %param.13), kind=kLoop, calls=%fused_computation.1 | loop fusion | flops 47 | bytes 68 | tf_op jit(solution)/shard_map/reduce_sum | solution.py:577
  1.9 0.0 copy-start
  2.0 0.6 copy-done
  2.6 115.5 %conditional.1 = (bf16[12,16,2560]{2,1,0:T(8,128)(2,1)S(1)}) conditional(s32[]{:T(128)} %convert_element_type.7, (s32[16]{0:T(128)S(1)}, bf16[12,16,2560]{2,1,0:T(8,128)(2,1)}, bf16[12,16,2560]{2,1,0:T(8,128)(2,1)}, bf16[12,16,2560]{2,1,0:T(8,128)(2,1)}, f32[2560]{0:T(1024)}, /*index=5*/f32[2560]{0:T(1024)}) %tuple.20, (s32[16]{0:T(128)S(1)}, ...), branch_computations={%region_1.0_spmd, %region_2.0_spmd} | conditional | bytes 8 | solution.py:578
  2.6 115.1 %attend_12.1 = bf16[12,16,2560]{2,1,0:T(8,128)(2,1)S(1)} custom-call(s32[16]{0:T(128)S(1)} %get-tuple-element.38.len_ref, bf16[12,16,2560]{2,1,0:T(8,128)(2,1)} %get-tuple-element.39.q_ref, bf16[12,16,2560]{2,1,0:T(8,128)(2,1)} %get-tuple-element.40.k_ref, bf16[12,16,2560]{2,1,0:T(8,128)(2,1)} %get-tuple-element.41.v_ref, f32[2560]{0:T(1024)} %get-tuple-element.42.qg_ref, ...), custom_call_target="tpu_custom_call" | custom-call | tf_op jit(solution)/shard_map/cond/branch_1_fun/attend_12/pallas_call | solution.py:555
  118.1 0.9 copy.10
Async XLA Ops:
  1.9 0.7 copy-start
